TPU v7x, 32 devices: a whole 2x2x4 slice. The times are simulated.
32 devices in a mesh: groups: 2 (over y), seq: 4 (over z), mp: 2 (over x), rep: 2 (over core).
Axes of the slice: x: 2, y: 2, z: 4, core: 2. Of those that a mesh axis runs over, the one named last changes fastest.
Arguments:
- tokens: bfloat16 [8192, 2240], P(('groups', 'seq', 'rep')), parts along dimension 0, may hold values from -8 to 8
- slot_image: int32 [32], P(('groups', 'seq', 'rep')), parts along dimension 0, may hold values from 0 to 5, as said below
- modulation: float32 [12, 3, 2240], P('groups'), parts along dimension 0, may hold values from -3 to 3
- w_qkv: bfloat16 [2240, 3, 1280], P('rep', None, 'mp'), may hold values from -0.125 to 0.125
- w_out: bfloat16 [1280, 2240], P('rep', 'mp'), may hold values from -0.15625 to 0.15625
Outputs:
- updated: bfloat16 [8192, 2240], P(('groups', 'seq', 'rep'), 'mp'), parts along dimension 0
There are 2 independent parts, one for each index of `groups`. A program takes and returns all parts, laid end to end along the dimension named above; an argument that names none is the same for every part. Nothing has to cross between parts.
Inputs may be any that keep to these rules, and one draw needn't show every extreme that they name: `slot_image`: every one of the 6 images owns one tile slot or more.
All inputs are finite; a program needn't handle non-finite values.
Results may differ from a plain program's by a relative error of at most 0.0036.
Values may be sent and summed in bfloat16 or wider, within the bound.
A program may use at most 128 MiB of HBM per device.

v0:
```python
import jax
import jax.numpy as jnp
from jax import lax
from jax.sharding import PartitionSpec as P

D = 2240
HD = 32


def body(tokens, slot_image, modulation, w_qkv, w_out):
    hi = lax.Precision.HIGHEST
    tiles = slot_image.shape[0]
    rows = tokens.shape[0]
    tile_len = rows // tiles
    images = modulation.shape[0]
    width = w_qkv.shape[2]
    per_dev = width // HD
    picker = (slot_image[:, None] == jnp.arange(images, dtype=jnp.int32)[None, :]).astype(
        jnp.float32
    )
    per_tile = jnp.dot(picker, modulation.reshape(images, 3 * D), precision=hi).reshape(tiles, 3, D)
    xf = tokens.astype(jnp.float32).reshape(tiles, tile_len, D)
    mean = jnp.mean(xf, axis=2, keepdims=True)
    var = jnp.mean((xf - mean) ** 2, axis=2, keepdims=True)
    normed = (xf - mean) / jnp.sqrt(var + 1e-06)
    modulated = (normed * (1.0 + per_tile[:, None, 1, :]) + per_tile[:, None, 0, :]).astype(
        jnp.bfloat16
    )
    modulated = modulated.reshape(rows, D)
    qkv = jnp.einsum(
        "td,dcm->tcm",
        modulated,
        lax.all_gather(w_qkv, "rep", axis=0, tiled=True),
        preferred_element_type=jnp.float32,
    )
    qkv = qkv.reshape(tiles, tile_len, 3, per_dev, HD)
    query = jax.nn.relu(qkv[:, :, 0]).astype(jnp.bfloat16)
    keyf = jax.nn.relu(qkv[:, :, 1]).astype(jnp.bfloat16)
    value = qkv[:, :, 2].astype(jnp.bfloat16)
    tile_state = jnp.einsum("slhe,slhf->shef", keyf, value, preferred_element_type=jnp.float32)
    tile_ksum = jnp.sum(keyf.astype(jnp.float32), axis=1)
    state = jnp.einsum("si,shef->ihef", picker, tile_state, precision=hi)
    ksum = jnp.einsum("si,she->ihe", picker, tile_ksum, precision=hi)
    state, ksum = lax.psum((state, ksum), ("seq", "rep"))
    own_state = jnp.einsum("si,ihef->shef", picker, state, precision=hi)
    own_ksum = jnp.einsum("si,ihe->she", picker, ksum, precision=hi)
    query_wide = query.astype(jnp.float32)
    numer = jnp.einsum("slhe,shef->slhf", query_wide, own_state, precision=hi)
    denom = jnp.einsum("slhe,she->slh", query_wide, own_ksum, precision=hi) + 1e-06
    attn = (numer / denom[..., None]).astype(jnp.bfloat16).reshape(rows, per_dev * HD)
    out_full = lax.all_gather(w_out, "rep", axis=0, tiled=True)
    cols = out_full.shape[1]
    projected = jnp.dot(
        lax.all_gather(attn, "mp", axis=1, tiled=True), out_full, preferred_element_type=jnp.float32
    )
    offset = lax.axis_index("mp") * cols
    own_tokens = (
        lax.dynamic_slice_in_dim(tokens, offset, cols, 1)
        .astype(jnp.float32)
        .reshape(tiles, tile_len, cols)
    )
    gate = lax.dynamic_slice_in_dim(per_tile[:, 2, :], offset, cols, 1)
    updated = own_tokens + gate[:, None, :] * projected.reshape(tiles, tile_len, cols)
    return updated.astype(jnp.bfloat16).reshape(rows, cols)


def solution(mesh):
    return jax.shard_map(
        body,
        mesh=mesh,
        in_specs=(
            P(("groups", "seq", "rep"), None),
            P(("groups", "seq", "rep")),
            P("groups", None, None),
            P("rep", None, "mp"),
            P("rep", "mp"),
        ),
        out_specs=P(("groups", "seq", "rep"), "mp"),
        check_vma=False,
    )
```

profile of v0, /device:TPU:0, one launch (start us, length us, event | category | flops | bytes accessed | tf_op | source)
XLA Modules:
  0.0 175.1 jit_solution(10275999285317942195)
XLA Ops:
  6.5 0.7 all-gather.4.cloned.1.call-update
  8.5 2.7 %mul.34 = f32[2,256,2240]{1,0,2:T(2,128)S(1)} broadcast(f32[2,2240]{0,1:T(8,128)S(1)} %copy.12), dimensions={0,2} | broadcast | bytes 4605440 | tf_op jit(solution)/shard_map/mul | solution.py:26
  11.3 2.6 %copy.34 = f32[280,8,2,256]{3,1,2,0:T(8,128)} copy(f32[280,8,2,256]{3,2,1,0:T(2,128)S(1)} %bitcast.80) | data formatting | bytes 9175040
  14.2 2.7 %add.57 = f32[2,256,2240]{1,0,2:T(2,128)S(1)} broadcast(f32[2,2240]{0,1:T(8,128)S(1)} %copy.13), dimensions={0,2} | broadcast | bytes 4605440 | tf_op jit(solution)/shard_map/add | solution.py:26
  17.5 1.5 copy-done
  20.1 3.0 %fusion.5 = bf16[512,2240]{0,1:T(8,128)(2,1)} fusion(f32[512,2240]{0,1:T(8,128)S(1)} %bitcast.79, f32[512,2240]{0,1:T(8,128)S(1)} %bitcast.78, bf16[512,2240]{0,1:T(8,128)(2,1)S(1)} %copy-done, f32[512]{0:T(512)S(1)} %add_sqrt_fusion, f32[512]{0:T(512)S(1)} %broadcast_multiply_fusion), kind=kLoop, calls=%fused_computation.7 | loop fusion | flops 6881280 | bytes 13766656 | tf_op jit(solution)/shard_map/convert_element_type | solution.py:26
  23.1 6.1 %dot_general.43 = bf16[2,256,2240]{1,0,2:T(2,128)(2,1)} reshape(bf16[512,2240]{0,1:T(8,128)(2,1)} %fusion.5) | data formatting | bytes 4587520 | tf_op jit(solution)/shard_map/td,dcm->tcm/dot_general | solution.py:30
  29.2 2.0 %all-gather.4.cloned.1.call-done = bf16[2240,3,640]{2,0,1:T(8,128)(2,1)} async-done(((bf16[1120,3,640]{2,0,1:T(8,128)(2,1)}), bf16[2240,3,640]{2,0,1:T(8,128)(2,1)}) %all-gather.4.cloned.1.call-update) | async-done | bytes 8601616 | tf_op jit(solution)/shard_map/all_gather | solution.py:33
  31.1 13.2 %copy.14 = bf16[3,640,2240]{2,1,0:T(8,128)(2,1)} copy(bf16[3,640,2240]{1,2,0:T(8,128)(2,1)} %bitcast.84) | data formatting | bytes 17203200 | tf_op jit(solution)/shard_map/td,dcm->tcm/dot_general | solution.py:30
  44.4 8.9 %fusion.10 = bf16[2,256,3,20,32]{1,4,3,2,0:T(8,128)(2,1)S(1)} fusion(bf16[3,20,32,2240,1]{3,2,1,0,4:T(8,128)(2,1)} %bitcast.83, bf16[2,256,2240,1,1]{1,0,2,4,3:T(2,128)(2,1)} %bitcast.88), kind=kOutput, calls=%fused_computation.13 | convolution fusion | flops 4404019200 | bytes 12861440 | tf_op jit(solution)/shard_map/td,dcm->tcm/dot_general | solution.py:30
  53.6 1.9 %fusion.22 = f32[6,20,32,32]{3,0,2,1:T(8,128)S(1)} fusion(f32[2,20,32,32]{3,2,1,0:T(8,128)S(1)} %fusion.18, s32[2]{0:T(128)S(1)} %copy-done.3), kind=kOutput, calls=%fused_computation.30 | convolution fusion | flops 2949132 | bytes 655368 | tf_op jit(solution)/shard_map/si,shef->ihef/dot_general | solution.py:42
  55.6 1.7 copy.20
  58.1 1.3 convert_reduce_fusion.1
  59.8 31.4 %psum.15 = f32[6,20,32]{2,1,0:T(8,128)S(1)} all-reduce(f32[6,20,32]{2,1,0:T(8,128)S(1)} %copy.24), channel_id=1, replica_groups=mesh['groups'=2,'seq'=4,'mp'=2,'rep'=2] {'seq','rep'}, use_global_device_ids=true, to_apply=%region_4.5 | all-reduce | flops 3840 | bytes 30720 | tf_op jit(solution)/shard_map/psum | solution.py:44
  91.4 1.5 fusion.27
  92.9 30.4 %all-reduce.2.cloned.1.call-done = f32[6,20,32,32]{3,2,1,0:T(8,128)} async-done(((f32[6,20,32,32]{3,2,1,0:T(8,128)}), f32[6,20,32,32]{3,2,1,0:T(8,128)}) %all-reduce.2.cloned.1.call-update) | async-done | bytes 491536 | tf_op jit(solution)/shard_map/psum | solution.py:44
  123.3 3.9 %fusion.8 = f32[2,20,32,32]{3,0,2,1:T(2,128)S(1)} fusion(f32[6,20,32,32]{3,2,1,0:T(8,128)} %all-reduce.2.cloned.1.call-done, s32[2]{0:T(128)S(1)} %copy-done.3), kind=kOutput, calls=%fused_computation.11 | convolution fusion | flops 2949132 | bytes 655368 | tf_op jit(solution)/shard_map/si,ihef->shef/dot_general | solution.py:45
  127.3 1.9 %fusion.13 = bf16[2,256,20,32]{1,3,2,0:T(8,128)(2,1)S(1)} fusion(f32[2,20,32,32]{3,0,2,1:T(2,128)S(1)} %fusion.8, f32[2,256,20]{1,2,0:T(8,128)S(1)} %fusion.31, bf16[2,256,3,20,32]{1,4,3,2,0:T(8,128)(2,1)} %copy-done.2), kind=kOutput, calls=%fused_computation.17 | convolution fusion | flops 127467520 | bytes 1515520 | tf_op jit(solution)/shard_map/slhe,shef->slhf/dot_general | solution.py:48
  129.8 0.9 copy.36
  131.1 1.3 mul.31
  132.5 1.6 copy.33
  134.1 2.0 %all-gather.8.cloned.1.call-done = bf16[1280,1120]{0,1:T(8,128)(2,1)} async-done(((bf16[640,1120]{0,1:T(8,128)(2,1)}), bf16[1280,1120]{0,1:T(8,128)(2,1)}) %all-gather.8.cloned.1.call-update) | async-done | bytes 2867216 | tf_op jit(solution)/shard_map/all_gather | solution.py:51
  136.1 26.9 %all-gather.6.cloned.1.call-done = bf16[512,1280]{0,1:T(8,128)(2,1)} async-done(((bf16[512,640]{0,1:T(8,128)(2,1)}), bf16[512,1280]{0,1:T(8,128)(2,1)}) %all-gather.6.cloned.1.call-update) | async-done | bytes 1310736 | tf_op jit(solution)/shard_map/all_gather | solution.py:54
  163.0 5.6 %fusion.7 = bf16[512,1120]{0,1:T(8,128)(2,1)} fusion(f32[512,1120]{0,1:T(8,128)} %bitcast.87, bf16[1280,1120]{0,1:T(8,128)(2,1)} %all-gather.8.cloned.1.call-done, bf16[512,1280]{0,1:T(8,128)(2,1)} %all-gather.6.cloned.1.call-done, bf16[512,2240]{0,1:T(8,128)(2,1)S(1)} %copy-done, s32[]{:T(128)S(6)} %select_n.4), kind=kOutput, calls=%fused_computation.10 | convolution fusion | flops 1470300160 | bytes 8765444 | tf_op jit(solution)/shard_map/dot_general | solution.py:53
  (38 shorter events, 5.8 us)
Async XLA Ops:
  6.5 0.9 copy-start.1
  6.5 24.6 %all-gather.4.cloned.1.call-start = ((), (), s32[]{:S(2)}) async-start(), calls=%async_computation | async-start | bytes 12902400 | tf_op jit(solution)/shard_map/all_gather | solution.py:33
  6.5 1.3 copy-start.3
  7.3 116.1 %all-reduce.2.cloned.1.call-start = ((), (), s32[]{:S(2)}) async-start(), calls=%async_computation.1 | async-start | bytes 3932160 | tf_op jit(solution)/shard_map/psum | solution.py:44
  14.2 5.9 %slice-start = ((s8[4587520]{0:T(1024)(128)(4,1)}), s8[4194304]{0:T(1024)(128)(4,1)S(1)}, s32[]{:S(2)}) async-start(s8[4587520]{0:T(1024)(128)(4,1)} %bitcast.76), calls=%async_computation.4 | async-start | bytes 8388608
  17.0 2.1 %copy-start = (bf16[512,2240]{0,1:T(8,128)(2,1)S(1)}, bf16[512,2240]{0,1:T(8,128)(2,1)}, u32[]{:S(2)}) copy-start(bf16[512,2240]{0,1:T(8,128)(2,1)} %param.5) | copy-start | bytes 6881284
  17.0 3.1 %slice-start.1 = ((s8[4587520]{0:T(1024)(128)(4,1)}), s8[393216]{0:T(1024)(128)(4,1)S(1)}, s32[]{:S(2)}) async-start(s8[4587520]{0:T(1024)(128)(4,1)} %bitcast.76), calls=%async_computation.5 | async-start | bytes 786432
  53.3 2.3 %copy-start.2 = (bf16[2,256,3,20,32]{1,4,3,2,0:T(8,128)(2,1)}, bf16[2,256,3,20,32]{1,4,3,2,0:T(8,128)(2,1)S(1)}, u32[]{:S(2)}) copy-start(bf16[2,256,3,20,32]{1,4,3,2,0:T(8,128)(2,1)S(1)} %fusion.10) | copy-start | bytes 5898244
  57.3 78.7 %all-gather.8.cloned.1.call-start = ((), (), s32[]{:S(2)}) async-start(), calls=%async_computation.3 | async-start | bytes 4300800 | tf_op jit(solution)/shard_map/all_gather | solution.py:51
  58.1 104.9 %all-gather.6.cloned.1.call-start = ((), (), s32[]{:S(2)}) async-start(), calls=%async_computation.2 | async-start | bytes 1966080 | tf_op jit(solution)/shard_map/all_gather | solution.py:54
Sparse Core Ops, SparseCore 0:
  8.9 22.1 all-gather.3
  57.4 65.8 all-reduce.1
  124.9 11.0 all-gather.7
  137.5 25.4 all-gather.5
where the time goes:
time: 176 us; the launch traced here: 175 us
  waiting for transfers between devices  62.7 us (36%)
  local copies, waits for them, and re-layouts  37.3 us (21%)
  blocking collectives  31.4 us (18%)
  matrix products  24.9 us (14%)
  between operations  13.3 us (8%)
  other arithmetic  5.39 us (3%)
    psum x1, blocking collectives, body(): state, ksum = lax.psum((state, ksum), ('seq', 'rep'))  31.4 us
    psum x1, waiting for transfers between devices, body(): state, ksum = lax.psum((state, ksum), ('seq', 'rep'))  30.4 us
    all_gather x1, waiting for transfers between devices, body(): lax.all_gather(attn, 'mp', axis=1, tiled=True)  26.9 us
    dot_general x2, local copies, waits for them, and re-layouts, body(): jnp.einsum('td,dcm->tcm', modulated, lax.all_gather(w_qkv, 'rep', axis=0,...  19.3 us
    dot_general x1, matrix products, body(): jnp.einsum('td,dcm->tcm', modulated, lax.all_gather(w_qkv, 'rep', axis=0,...  8.94 us
    unnamed x16, local copies, waits for them, and re-layouts  7.35 us
    dot_general x1, matrix products, body(): jnp.dot(lax.all_gather(attn, 'mp', axis=1, tiled=True), out_full, preferr...  5.59 us
    dot_general x1, matrix products, body(): own_state = jnp.einsum('si,ihef->shef', picker, state, precision=hi)  3.93 us
  transfers between devices with their start and end apart: 4, of which 4 were waited for; matrix products, arithmetic and copies ran while one was open for 19% of the time, Pallas kernels for 0%

commit v1 on v0

--- a/solution.py
+++ b/solution.py
@@ -1,6 +1,10 @@
+import functools
+
 import jax
 import jax.numpy as jnp
 from jax import lax
+from jax.experimental import pallas as pl
+from jax.experimental.pallas import tpu as pltpu
 from jax.sharding import PartitionSpec as P
 
 D = 2240
@@ -64,9 +68,301 @@
     return updated.astype(jnp.bfloat16).reshape(rows, cols)
 
 
+MESH = pl.DeviceIdType.MESH
+LANES = 128
+NT = (((1,), (1,)), ((), ()))
+TN = (((0,), (0,)), ((), ()))
+
+
+def fused_kernel(
+    nz, slot_ref, mod_ref, tok_hbm, w_hbm, wo_hbm, out_ref,
+    tok, w, wo, modulated, q, k, v, att, gate, st, own,
+    loc_sem, w_send, w_recv, q_send, q_recv, z_send, z_recv, f_send, f_recv, x_send, x_recv,
+):
+    f32, bf16 = jnp.float32, jnp.bfloat16
+    z, m, r = lax.axis_index("seq"), lax.axis_index("mp"), lax.axis_index("rep")
+    half, width = w_hbm.shape[1], w_hbm.shape[2]
+    tiles = slot_ref.shape[0]
+    tile_len = tok.shape[1] // tiles
+    blocks = width // LANES
+    out_rows = out_ref.shape[0]
+    core, other_x = {"rep": 1 - r}, {"mp": 1 - m}
+
+    def remote(src, dst, send, recv, device):
+        return pltpu.make_async_remote_copy(
+            src_ref=src, dst_ref=dst, send_sem=send, recv_sem=recv,
+            device_id=device, device_id_type=MESH,
+        )
+
+    local = [pltpu.make_async_copy(tok_hbm, tok, loc_sem.at[0])]
+    for c in range(3):
+        local.append(pltpu.make_async_copy(w_hbm.at[c], w.at[r, c], loc_sem.at[1 + c]))
+    local.append(pltpu.make_async_copy(wo_hbm, wo.at[r], loc_sem.at[4]))
+    for copy in local:
+        copy.start()
+
+    barrier = pltpu.get_barrier_semaphore()
+    pl.semaphore_signal(barrier, inc=1, device_id=core, device_id_type=MESH)
+    pl.semaphore_signal(barrier, inc=1, device_id=other_x, device_id_type=MESH)
+    for d in range(1, nz):
+        pl.semaphore_signal(
+            barrier, inc=1, device_id={"seq": lax.rem(z + d, nz)}, device_id_type=MESH
+        )
+    pl.semaphore_wait(barrier, nz + 1)
+
+    weights = [remote(w_hbm.at[c], w.at[r, c], w_send.at[c], w_recv.at[c], core) for c in range(3)]
+    weights.append(remote(wo_hbm, wo.at[r], w_send.at[3], w_recv.at[3], core))
+    for copy in weights:
+        copy.start()
+
+    eye = (
+        lax.broadcasted_iota(jnp.int32, (tile_len, tile_len), 0)
+        == lax.broadcasted_iota(jnp.int32, (tile_len, tile_len), 1)
+    ).astype(bf16)
+    local[0].wait()
+    for t in range(tiles):
+        rows = slice(t * tile_len, (t + 1) * tile_len)
+        table = mod_ref[slot_ref[t]]
+        x = [
+            lax.dot_general(
+                eye, tok[h * half : (h + 1) * half, rows], NT, preferred_element_type=f32
+            )
+            for h in range(2)
+        ]
+        mean = (
+            jnp.sum(x[0], axis=1, keepdims=True) + jnp.sum(x[1], axis=1, keepdims=True)
+        ) / (2 * half)
+        x = [y - mean for y in x]
+        var = (
+            jnp.sum(x[0] * x[0], axis=1, keepdims=True)
+            + jnp.sum(x[1] * x[1], axis=1, keepdims=True)
+        ) / (2 * half)
+        scale = 1.0 / jnp.sqrt(var + 1e-06)
+        for h in range(2):
+            cols = slice(h * half, (h + 1) * half)
+            modulated[h, rows, :] = (
+                x[h] * scale * (1.0 + table[1:2, cols]) + table[0:1, cols]
+            ).astype(bf16)
+
+    def project(c, t):
+        rows = slice(t * tile_len, (t + 1) * tile_len)
+        return jnp.dot(modulated[0, rows, :], w[0, c], preferred_element_type=f32) + jnp.dot(
+            modulated[1, rows, :], w[1, c], preferred_element_type=f32
+        )
+
+    queries = []
+    for c in range(3):
+        local[1 + c].wait()
+        weights[c].wait()
+        for t in range(tiles):
+            rows = pl.ds(t * tile_len, tile_len)
+            y = project(c, t)
+            if c < 2:
+                y = jnp.maximum(y, 0.0)
+            y = y.astype(bf16)
+            if c == 0:
+                q[m, rows, :] = y
+                copy = remote(
+                    q.at[m, rows], q.at[m, rows], q_send.at[t], q_recv.at[t], other_x
+                )
+                copy.start()
+                queries.append(copy)
+            elif c == 1:
+                k[rows, :] = y
+            else:
+                v[rows, :] = y
+
+    row = lax.broadcasted_iota(jnp.int32, (LANES, LANES), 0)
+    lane = lax.broadcasted_iota(jnp.int32, (LANES, LANES), 1)
+    group = (lane // HD - row // HD + 4) % 4
+    diagonal = group == 0
+    inner = lane % HD
+    zero = jnp.zeros((LANES, LANES), f32)
+    ones = jnp.ones((tile_len, LANES), bf16)
+    mine = 2 * z + r
+    last = zero
+    for t in range(tiles):
+        rows = slice(t * tile_len, (t + 1) * tile_len)
+        packed, sums = zero, zero
+        for b in range(blocks):
+            cols = slice(b * LANES, (b + 1) * LANES)
+            both = lax.dot_general(
+                k[rows, cols], jnp.concatenate([v[rows, cols], ones], axis=1), TN,
+                preferred_element_type=f32,
+            )
+            s = jnp.where(diagonal, both[:, :LANES], 0.0)
+            sums = jnp.where(jnp.logical_and(diagonal, inner == b), both[:, LANES:], sums)
+            if b == 0:
+                packed = s
+            elif b < 4:
+                packed = packed + pltpu.roll(s, HD * b, 1)
+            else:
+                last = last + (pltpu.roll(s, HD * t, 1) if t else s)
+        last = last + pltpu.roll(sums, HD * (2 + t), 1)
+        st[mine, t * LANES : (t + 1) * LANES, :] = packed.astype(bf16)
+    st[mine, 2 * LANES : 3 * LANES, :] = last.astype(bf16)
+    images = [jnp.full((8, LANES), slot_ref[t], jnp.int32).astype(f32) for t in range(tiles)]
+    st[mine, 3 * LANES : 3 * LANES + 16, :] = jnp.concatenate(images, axis=0).astype(bf16)
+
+    across = []
+    for d in range(1, nz):
+        across.append(
+            remote(
+                st.at[mine], st.at[mine], z_send.at[d], z_recv.at[d],
+                {"seq": lax.rem(z + d, nz)},
+            )
+        )
+        across[-1].start()
+    forwards = [remote(st.at[mine], st.at[mine], f_send.at[0], f_recv.at[0], core)]
+    forwards[0].start()
+
+    for t in range(tiles):
+        table = mod_ref[slot_ref[t]]
+        for start in range(0, 2 * half, LANES):
+            stop = min(start + LANES, 2 * half)
+            gate[t, start:stop, :] = jnp.broadcast_to(
+                table[2:3, start:stop], (LANES, stop - start)
+            ).T
+
+    for d in range(1, nz):
+        across[d - 1].wait_recv()
+        source = 2 * lax.rem(z - d + nz, nz) + r
+        forwards.append(
+            remote(st.at[source], st.at[source], f_send.at[d], f_recv.at[d], core)
+        )
+        forwards[d].start()
+    for copy in forwards:
+        copy.wait_recv()
+
+    even = group % 2 == 0
+    pair = zero
+    for t in range(tiles):
+        target = images[t][0:1]
+
+        def gather(i, carry, target=target):
+            a, c = carry
+            ids = st[i, 3 * LANES : 3 * LANES + 16, :].astype(f32)
+            first = jnp.where(ids[0:1] == target, 1.0, 0.0)
+            second = jnp.where(ids[8:9] == target, 1.0, 0.0)
+            a = a + first * st[i, 0:LANES, :].astype(f32)
+            a = a + second * st[i, LANES : 2 * LANES, :].astype(f32)
+            c = c + jnp.where(even, first, second) * st[i, 2 * LANES : 3 * LANES, :].astype(f32)
+            return a, c
+
+        a, c = lax.fori_loop(0, 2 * nz, gather, (zero, zero))
+        own[m, t * LANES : (t + 1) * LANES, :] = a.astype(bf16)
+        c = jnp.where(even, c + pltpu.roll(c, LANES - HD, 1), 0.0)
+        pair = pair + (pltpu.roll(c, HD * t, 1) if t else c)
+    own[m, 2 * LANES : 3 * LANES, :] = pair.astype(bf16)
+    states = remote(own.at[m], own.at[m], x_send.at[0], x_recv.at[0], other_x)
+    states.start()
+
+    def attend(j):
+        rest = own[j, 2 * LANES : 3 * LANES, :].astype(f32)
+        for t in range(tiles):
+            rows = slice(t * tile_len, (t + 1) * tile_len)
+            packed = own[j, t * LANES : (t + 1) * LANES, :].astype(f32)
+            sums = jnp.where(diagonal, pltpu.roll(rest, LANES - HD * (2 + t), 1), 0.0)
+            for b in range(blocks):
+                cols = slice(b * LANES, (b + 1) * LANES)
+                if b < 4:
+                    s = pltpu.roll(packed, LANES - HD * b, 1) if b else packed
+                else:
+                    s = pltpu.roll(rest, LANES - HD * t, 1) if t else rest
+                s = jnp.where(diagonal, s, 0.0)
+                ksum = jnp.sum(jnp.where(inner == b, sums, 0.0), axis=1, keepdims=True)
+                ksum = jnp.where(diagonal, ksum, 0.0)
+                both = jnp.dot(
+                    q[j, rows, cols], jnp.concatenate([s, ksum], axis=1).astype(bf16),
+                    preferred_element_type=f32,
+                )
+                att[j, rows, cols] = (both[:, :LANES] / (both[:, LANES:] + 1e-06)).astype(bf16)
+
+    attend(m)
+    local[4].wait()
+    weights[3].wait()
+    for copy in queries:
+        copy.wait()
+    states.wait()
+    attend(1 - m)
+
+    step = out_rows // 2
+    for t in range(tiles):
+        rows = slice(t * tile_len, (t + 1) * tile_len)
+        for start in range(0, out_rows, step):
+            part = pl.ds(pl.multiple_of(m * out_rows + start, 16), step)
+            projected = lax.dot_general(
+                wo[0, start : start + step, :], att[0, rows, :], NT, preferred_element_type=f32
+            ) + lax.dot_general(
+                wo[1, start : start + step, :], att[1, rows, :], NT, preferred_element_type=f32
+            )
+            g = gate[t, part, :]
+            g = jnp.concatenate([g] * (tile_len // LANES), axis=1)
+            out_ref[start : start + step, rows] = (
+                tok[part, rows].astype(f32) + g * projected
+            ).astype(bf16)
+    for copy in across + forwards:
+        copy.wait_send()
+
+
+def fused(nz, tokens, slot_image, modulation, w_qkv, w_out):
+    rows, d = tokens.shape
+    half, _, width = w_qkv.shape
+    cols = w_out.shape[1]
+    tiles = slot_image.shape[0]
+    bf16 = jnp.bfloat16
+    any_spec = pl.BlockSpec(memory_space=pl.ANY)
+    dma = pltpu.SemaphoreType.DMA
+    out = pl.pallas_call(
+        functools.partial(fused_kernel, nz),
+        out_shape=jax.ShapeDtypeStruct((cols, rows), bf16),
+        in_specs=[
+            pl.BlockSpec(memory_space=pltpu.SMEM),
+            pl.BlockSpec(memory_space=pltpu.VMEM),
+            any_spec,
+            any_spec,
+            any_spec,
+        ],
+        out_specs=pl.BlockSpec(memory_space=pltpu.VMEM),
+        scratch_shapes=[
+            pltpu.VMEM((d, rows), bf16),
+            pltpu.VMEM((2, 3, half, width), bf16),
+            pltpu.VMEM((2, cols, width), bf16),
+            pltpu.VMEM((2, rows, half), bf16),
+            pltpu.VMEM((2, rows, width), bf16),
+            pltpu.VMEM((rows, width), bf16),
+            pltpu.VMEM((rows, width), bf16),
+            pltpu.VMEM((2, rows, width), bf16),
+            pltpu.VMEM((tiles, d, LANES), jnp.float32),
+            pltpu.VMEM((2 * nz, 3 * LANES + 16, LANES), bf16),
+            pltpu.VMEM((2, 3 * LANES, LANES), bf16),
+            dma((5,)), dma((4,)), dma((4,)), dma((tiles,)), dma((tiles,)),
+            dma((nz,)), dma((nz,)), dma((nz,)), dma((nz,)), dma((1,)), dma((1,)),
+        ],
+        compiler_params=pltpu.CompilerParams(
+            collective_id=0, has_side_effects=True, vmem_limit_bytes=56 * 1024 * 1024
+        ),
+    )(slot_image, modulation, tokens.T, jnp.transpose(w_qkv, (1, 0, 2)), w_out.T)
+    return out.T
+
+
+def choose(nz, mp, reps, tokens, slot_image, modulation, w_qkv, w_out):
+    rows, d = tokens.shape
+    half, _, width = w_qkv.shape
+    tiles = slot_image.shape[0]
+    fits = (
+        mp == 2 and reps == 2 and tiles == 2 and width == 5 * LANES
+        and w_out.shape[0] == width and LANES % HD == 0 and modulation.shape[0] <= 256
+        and (rows // tiles) % LANES == 0 and half % 16 == 0 and w_out.shape[1] % 32 == 0
+    )
+    if fits:
+        return fused(nz, tokens, slot_image, modulation, w_qkv, w_out)
+    return body(tokens, slot_image, modulation, w_qkv, w_out)
+
+
 def solution(mesh):
     return jax.shard_map(
-        body,
+        functools.partial(choose, mesh.shape["seq"], mesh.shape["mp"], mesh.shape["rep"]),
         mesh=mesh,
         in_specs=(
             P(("groups", "seq", "rep"), None),

time: 176 us -> 37.9 us (0.22)
  waiting for transfers between devices: 62.7 us -> 0 us
  Pallas kernels: 0 us -> 35.4 us
  local copies, waits for them, and re-layouts: 37.3 us -> 2.34 us
  blocking collectives: 31.4 us -> 0 us
  matrix products: 24.9 us -> 0 us
  between operations: 13.3 us -> 0.01 us
  other arithmetic: 5.39 us -> 0 us
    pallas_call x0 -> x1, Pallas kernels: none -> 35.4 us  [fused(): pl.pallas_call(functools.partial(fused_kernel, nz), out_shape=jax.ShapeDt...]
    psum x1 -> x0, blocking collectives: 31.4 us -> none  [body(): state, ksum = lax.psum((state, ksum), ('seq', 'rep'))]
    all_gather x3 -> x0, waiting for transfers between devices: 30.9 us -> none  [the longest x1 26.9 us: body(): lax.all_gather(attn, 'mp', axis=1, tiled=True)]
    psum x1 -> x0, waiting for transfers between devices: 30.4 us -> none  [body(): state, ksum = lax.psum((state, ksum), ('seq', 'rep'))]
    dot_general x10 -> x0, matrix products: 24.9 us -> none  [the longest x1 8.94 us: body(): jnp.einsum('td,dcm->tcm', modulated, lax.all_gather(w_qkv, 'rep', axis=0,...]
    dot_general x5 -> x0, local copies, waits for them, and re-layouts: 21.2 us -> none  [the longest x2 19.3 us: body(): jnp.einsum('td,dcm->tcm', modulated, lax.all_gather(w_qkv, 'rep', axis=0,...]
    unnamed x16 -> x1, local copies, waits for them, and re-layouts: 7.35 us -> 2.34 us
    mul x5 -> x0, local copies, waits for them, and re-layouts: 4.79 us -> none  [the longest x2 3.12 us: body(): normed * (1.0 + per_tile[:, None, 1, :]) + per_tile[:, None, 0, :]]
  transfers between devices with their start and end apart: 4 -> 0, of which waited for: 4 -> 0; matrix products, arithmetic and copies ran while one was open for 19% -> 0% of each run, Pallas kernels for 0% -> 0%
where the time goes in v1:
time: 37.9 us; the launch traced here: 37.7 us
  Pallas kernels  35.4 us (93%)
  local copies, waits for them, and re-layouts  2.34 us (6%)
    pallas_call x1, Pallas kernels, fused(): pl.pallas_call(functools.partial(fused_kernel, nz), out_shape=jax.ShapeDt...  35.4 us
    unnamed x1, local copies, waits for them, and re-layouts  2.34 us

profile of v1, /device:TPU:0, one launch (start us, length us, event | category | flops | bytes accessed | tf_op | source)
XLA Modules:
  0.0 37.7 jit_solution(15649002138080546879)
XLA Ops:
  0.0 35.4 %shard_map.55 = bf16[1120,512]{1,0:T(8,128)(2,1)} custom-call(s32[2]{0:T(128)} %slot_ref.1, f32[6,3,2240]{2,1,0:T(4,128)} %mod_ref.1, bf16[2240,512]{1,0:T(8,128)(2,1)} %bitcast.6, bf16[3,1120,640]{2,1,0:T(8,128)(2,1)} %bitcast.5, bf16[1120,640]{1,0:T(8,128)(2,1)} %bitcast.7), custom_call_target="tpu_custom_call" | custom-call | tf_op jit(solution)/shard_map/pallas_call | solution.py:316
  35.4 2.3 %copy.7 = bf16[512,1120]{0,1:T(8,128)(2,1)} copy(bf16[512,1120]{0,1:T(8,128)(2,1)} %bitcast.4) | data formatting | bytes 2293760

commit v2 on v1

--- a/solution.py
+++ b/solution.py
@@ -76,8 +76,8 @@
 
 def fused_kernel(
     nz, slot_ref, mod_ref, tok_hbm, w_hbm, wo_hbm, out_ref,
-    tok, w, wo, modulated, q, k, v, att, gate, st, own,
-    loc_sem, w_send, w_recv, q_send, q_recv, z_send, z_recv, f_send, f_recv, x_send, x_recv,
+    tok, w, wo, modulated, q, k, v, att, gate, snd, st, res, own, acc,
+    loc_sem, w_send, w_recv, q_send, q_recv, z_send, z_recv, x_send, x_recv,
 ):
     f32, bf16 = jnp.float32, jnp.bfloat16
     z, m, r = lax.axis_index("seq"), lax.axis_index("mp"), lax.axis_index("rep")
@@ -101,26 +101,33 @@
     for copy in local:
         copy.start()
 
+    parts = 2 * nz
+    part = LANES // parts
+    mine = 2 * z + r
+
+    def member(d, e):
+        p = lax.rem(mine + d, parts)
+        return {"seq": p // 2, "rep": lax.rem(p, 2), "mp": lax.rem(m + e, 2)}
+
     barrier = pltpu.get_barrier_semaphore()
-    pl.semaphore_signal(barrier, inc=1, device_id=core, device_id_type=MESH)
-    pl.semaphore_signal(barrier, inc=1, device_id=other_x, device_id_type=MESH)
-    for d in range(1, nz):
-        pl.semaphore_signal(
-            barrier, inc=1, device_id={"seq": lax.rem(z + d, nz)}, device_id_type=MESH
-        )
-    pl.semaphore_wait(barrier, nz + 1)
+    for e in range(2):
+        for d in range(parts):
+            if d or e:
+                pl.semaphore_signal(
+                    barrier, inc=1, device_id=member(d, e), device_id_type=MESH
+                )
+    pl.semaphore_wait(barrier, 2 * parts - 1)
 
     weights = [remote(w_hbm.at[c], w.at[r, c], w_send.at[c], w_recv.at[c], core) for c in range(3)]
     weights.append(remote(wo_hbm, wo.at[r], w_send.at[3], w_recv.at[3], core))
-    for copy in weights:
-        copy.start()
+    weights[0].start()
 
     eye = (
         lax.broadcasted_iota(jnp.int32, (tile_len, tile_len), 0)
         == lax.broadcasted_iota(jnp.int32, (tile_len, tile_len), 1)
     ).astype(bf16)
     local[0].wait()
-    for t in range(tiles):
+    def normalize(t):
         rows = slice(t * tile_len, (t + 1) * tile_len)
         table = mod_ref[slot_ref[t]]
         x = [
@@ -150,27 +157,28 @@
             modulated[1, rows, :], w[1, c], preferred_element_type=f32
         )
 
+    local[1].wait()
     queries = []
-    for c in range(3):
+    for t in range(tiles):
+        rows = pl.ds(t * tile_len, tile_len)
+        normalize(t)
+        if t == 0:
+            weights[0].wait()
+            weights[1].start()
+            weights[2].start()
+        q[m, rows, :] = jnp.maximum(project(0, t), 0.0).astype(bf16)
+        queries.append(remote(q.at[m, rows], q.at[m, rows], q_send.at[t], q_recv.at[t], other_x))
+        queries[t].start()
+    for c, dest in ((1, k), (2, v)):
         local[1 + c].wait()
         weights[c].wait()
+        if c == 1:
+            weights[3].start()
         for t in range(tiles):
-            rows = pl.ds(t * tile_len, tile_len)
             y = project(c, t)
-            if c < 2:
+            if c == 1:
                 y = jnp.maximum(y, 0.0)
-            y = y.astype(bf16)
-            if c == 0:
-                q[m, rows, :] = y
-                copy = remote(
-                    q.at[m, rows], q.at[m, rows], q_send.at[t], q_recv.at[t], other_x
-                )
-                copy.start()
-                queries.append(copy)
-            elif c == 1:
-                k[rows, :] = y
-            else:
-                v[rows, :] = y
+            dest[t * tile_len : (t + 1) * tile_len, :] = y.astype(bf16)
 
     row = lax.broadcasted_iota(jnp.int32, (LANES, LANES), 0)
     lane = lax.broadcasted_iota(jnp.int32, (LANES, LANES), 1)
@@ -179,8 +187,8 @@
     inner = lane % HD
     zero = jnp.zeros((LANES, LANES), f32)
     ones = jnp.ones((tile_len, LANES), bf16)
-    mine = 2 * z + r
     last = zero
+    outgoing = []
     for t in range(tiles):
         rows = slice(t * tile_len, (t + 1) * tile_len)
         packed, sums = zero, zero
@@ -199,22 +207,22 @@
             else:
                 last = last + (pltpu.roll(s, HD * t, 1) if t else s)
         last = last + pltpu.roll(sums, HD * (2 + t), 1)
-        st[mine, t * LANES : (t + 1) * LANES, :] = packed.astype(bf16)
-    st[mine, 2 * LANES : 3 * LANES, :] = last.astype(bf16)
+        outgoing.append(packed.astype(bf16))
+    outgoing.append(last.astype(bf16))
     images = [jnp.full((8, LANES), slot_ref[t], jnp.int32).astype(f32) for t in range(tiles)]
-    st[mine, 3 * LANES : 3 * LANES + 16, :] = jnp.concatenate(images, axis=0).astype(bf16)
-
-    across = []
-    for d in range(1, nz):
-        across.append(
-            remote(
-                st.at[mine], st.at[mine], z_send.at[d], z_recv.at[d],
-                {"seq": lax.rem(z + d, nz)},
-            )
+    images = jnp.concatenate(images, axis=0).astype(bf16)
+    for i in range(parts):
+        for n in range(3):
+            snd[i, n * part : (n + 1) * part, :] = outgoing[n][i * part : (i + 1) * part]
+        snd[i, 3 * part : 3 * part + 16, :] = images
+    scatter = []
+    for d in range(1, parts):
+        p = lax.rem(mine + d, parts)
+        scatter.append(
+            remote(snd.at[p], st.at[mine], z_send.at[d], z_recv.at[d], member(d, 0))
         )
-        across[-1].start()
-    forwards = [remote(st.at[mine], st.at[mine], f_send.at[0], f_recv.at[0], core)]
-    forwards[0].start()
+        scatter[-1].start()
+    st[mine] = snd[mine]
 
     for t in range(tiles):
         table = mod_ref[slot_ref[t]]
@@ -224,44 +232,57 @@
                 table[2:3, start:stop], (LANES, stop - start)
             ).T
 
-    for d in range(1, nz):
-        across[d - 1].wait_recv()
-        source = 2 * lax.rem(z - d + nz, nz) + r
-        forwards.append(
-            remote(st.at[source], st.at[source], f_send.at[d], f_recv.at[d], core)
-        )
-        forwards[d].start()
-    for copy in forwards:
-        copy.wait_recv()
-
-    even = group % 2 == 0
-    pair = zero
-    for t in range(tiles):
-        target = images[t][0:1]
-
-        def gather(i, carry, target=target):
-            a, c = carry
-            ids = st[i, 3 * LANES : 3 * LANES + 16, :].astype(f32)
-            first = jnp.where(ids[0:1] == target, 1.0, 0.0)
-            second = jnp.where(ids[8:9] == target, 1.0, 0.0)
-            a = a + first * st[i, 0:LANES, :].astype(f32)
-            a = a + second * st[i, LANES : 2 * LANES, :].astype(f32)
-            c = c + jnp.where(even, first, second) * st[i, 2 * LANES : 3 * LANES, :].astype(f32)
-            return a, c
-
-        a, c = lax.fori_loop(0, 2 * nz, gather, (zero, zero))
-        own[m, t * LANES : (t + 1) * LANES, :] = a.astype(bf16)
-        c = jnp.where(even, c + pltpu.roll(c, LANES - HD, 1), 0.0)
-        pair = pair + (pltpu.roll(c, HD * t, 1) if t else c)
-    own[m, 2 * LANES : 3 * LANES, :] = pair.astype(bf16)
-    states = remote(own.at[m], own.at[m], x_send.at[0], x_recv.at[0], other_x)
-    states.start()
+    for copy in scatter:
+        copy.wait()
+
+    small_row = lax.broadcasted_iota(jnp.int32, (part, LANES), 0) + mine * part
+    small_lane = lax.broadcasted_iota(jnp.int32, (part, LANES), 1)
+    even = (small_lane // HD + small_row // HD) % 2 == 0
+
+    @pl.loop(0, parts)
+    def reduce(d):
+        p = lax.rem(mine + d, parts)
+        pair = None
+        for t in range(tiles):
+            target = st[p, 3 * part : 3 * part + 16, :].astype(f32)[8 * t : 8 * t + 1]
+            a = jnp.zeros((part, LANES), f32)
+            c = jnp.zeros((part, LANES), f32)
+            for i in range(parts):
+                block = st[i].astype(f32)
+                first = jnp.where(block[3 * part : 3 * part + 1] == target, 1.0, 0.0)
+                second = jnp.where(block[3 * part + 8 : 3 * part + 9] == target, 1.0, 0.0)
+                a = a + first * block[:part] + second * block[part : 2 * part]
+                c = c + jnp.where(even, first, second) * block[2 * part : 3 * part]
+            res[p, t * part : (t + 1) * part, :] = a.astype(bf16)
+            c = jnp.where(even, c + pltpu.roll(c, LANES - HD, 1), 0.0)
+            pair = pair + pltpu.roll(c, HD * t, 1) if t else c
+        res[p, 2 * part : 3 * part, :] = pair.astype(bf16)
+
+        @pl.when(d > 0)
+        def _():
+            remote(
+                res.at[p], own.at[m, mine], x_send.at[d], x_recv.at[d], member(d, 0)
+            ).start()
+
+    states = [[], []]
+    for e in range(2):
+        for d in range(parts):
+            if d or e:
+                p = lax.rem(mine + d, parts)
+                copy = remote(
+                    res.at[p], own.at[m, mine], x_send.at[parts * e + d],
+                    x_recv.at[parts * e + d], member(d, e),
+                )
+                if e:
+                    copy.start()
+                states[e].append(copy)
+    own[m, mine] = res[mine]
 
     def attend(j):
-        rest = own[j, 2 * LANES : 3 * LANES, :].astype(f32)
+        rest = own[j, :, 2 * part : 3 * part, :].astype(f32).reshape(LANES, LANES)
         for t in range(tiles):
             rows = slice(t * tile_len, (t + 1) * tile_len)
-            packed = own[j, t * LANES : (t + 1) * LANES, :].astype(f32)
+            packed = own[j, :, t * part : (t + 1) * part, :].astype(f32).reshape(LANES, LANES)
             sums = jnp.where(diagonal, pltpu.roll(rest, LANES - HD * (2 + t), 1), 0.0)
             for b in range(blocks):
                 cols = slice(b * LANES, (b + 1) * LANES)
@@ -278,31 +299,36 @@
                 )
                 att[j, rows, cols] = (both[:, :LANES] / (both[:, LANES:] + 1e-06)).astype(bf16)
 
+    step = out_rows // 2
+
+    def output(j, finish):
+        for t in range(tiles):
+            rows = slice(t * tile_len, (t + 1) * tile_len)
+            for start in range(0, out_rows, step):
+                here = slice(start, start + step)
+                part = pl.ds(pl.multiple_of(m * out_rows + start, 16), step)
+                projected = lax.dot_general(
+                    wo[j, here, :], att[j, rows, :], NT, preferred_element_type=f32
+                )
+                g = gate[t, part, :]
+                g = jnp.concatenate([g] * (tile_len // LANES), axis=1)
+                if finish:
+                    out_ref[here, rows] = (acc[here, rows] + g * projected).astype(bf16)
+                else:
+                    acc[here, rows] = tok[part, rows].astype(f32) + g * projected
+
+    for copy in states[0]:
+        copy.wait()
     attend(m)
     local[4].wait()
     weights[3].wait()
+    output(m, False)
     for copy in queries:
         copy.wait()
-    states.wait()
+    for copy in states[1]:
+        copy.wait()
     attend(1 - m)
-
-    step = out_rows // 2
-    for t in range(tiles):
-        rows = slice(t * tile_len, (t + 1) * tile_len)
-        for start in range(0, out_rows, step):
-            part = pl.ds(pl.multiple_of(m * out_rows + start, 16), step)
-            projected = lax.dot_general(
-                wo[0, start : start + step, :], att[0, rows, :], NT, preferred_element_type=f32
-            ) + lax.dot_general(
-                wo[1, start : start + step, :], att[1, rows, :], NT, preferred_element_type=f32
-            )
-            g = gate[t, part, :]
-            g = jnp.concatenate([g] * (tile_len // LANES), axis=1)
-            out_ref[start : start + step, rows] = (
-                tok[part, rows].astype(f32) + g * projected
-            ).astype(bf16)
-    for copy in across + forwards:
-        copy.wait_send()
+    output(1 - m, True)
 
 
 def fused(nz, tokens, slot_image, modulation, w_qkv, w_out):
@@ -310,6 +336,8 @@
     half, _, width = w_qkv.shape
     cols = w_out.shape[1]
     tiles = slot_image.shape[0]
+    parts = 2 * nz
+    part = LANES // parts
     bf16 = jnp.bfloat16
     any_spec = pl.BlockSpec(memory_space=pl.ANY)
     dma = pltpu.SemaphoreType.DMA
@@ -334,10 +362,13 @@
             pltpu.VMEM((rows, width), bf16),
             pltpu.VMEM((2, rows, width), bf16),
             pltpu.VMEM((tiles, d, LANES), jnp.float32),
-            pltpu.VMEM((2 * nz, 3 * LANES + 16, LANES), bf16),
-            pltpu.VMEM((2, 3 * LANES, LANES), bf16),
+            pltpu.VMEM((parts, 3 * part + 16, LANES), bf16),
+            pltpu.VMEM((parts, 3 * part + 16, LANES), bf16),
+            pltpu.VMEM((parts, 3 * part, LANES), bf16),
+            pltpu.VMEM((2, parts, 3 * part, LANES), bf16),
+            pltpu.VMEM((cols, rows), jnp.float32),
             dma((5,)), dma((4,)), dma((4,)), dma((tiles,)), dma((tiles,)),
-            dma((nz,)), dma((nz,)), dma((nz,)), dma((nz,)), dma((1,)), dma((1,)),
+            dma((parts,)), dma((parts,)), dma((2 * parts,)), dma((2 * parts,)),
         ],
         compiler_params=pltpu.CompilerParams(
             collective_id=0, has_side_effects=True, vmem_limit_bytes=56 * 1024 * 1024
@@ -351,7 +382,7 @@
     half, _, width = w_qkv.shape
     tiles = slot_image.shape[0]
     fits = (
-        mp == 2 and reps == 2 and tiles == 2 and width == 5 * LANES
+        nz in (1, 2, 4) and mp == 2 and reps == 2 and tiles == 2 and width == 5 * LANES
         and w_out.shape[0] == width and LANES % HD == 0 and modulation.shape[0] <= 256
         and (rows // tiles) % LANES == 0 and half % 16 == 0 and w_out.shape[1] % 32 == 0
     )

time: 37.9 us -> 35.9 us (0.947)
  Pallas kernels: 35.4 us -> 33.4 us
    pallas_call x1, Pallas kernels: 35.4 us -> 33.4 us  [fused(): pl.pallas_call(functools.partial(fused_kernel, nz), out_shape=jax.ShapeDt...]
where the time goes in v2:
time: 35.9 us; the launch traced here: 35.8 us
  Pallas kernels  33.4 us (93%)
  local copies, waits for them, and re-layouts  2.34 us (7%)
    pallas_call x1, Pallas kernels, fused(): pl.pallas_call(functools.partial(fused_kernel, nz), out_shape=jax.ShapeDt...  33.4 us
    unnamed x1, local copies, waits for them, and re-layouts  2.34 us

profile of v2, /device:TPU:0, one launch (start us, length us, event | category | flops | bytes accessed | tf_op | source)
XLA Modules:
  0.0 35.8 jit_solution(11977352678549973279)
XLA Ops:
  0.0 33.4 %shard_map.55 = bf16[1120,512]{1,0:T(8,128)(2,1)} custom-call(s32[2]{0:T(128)} %slot_ref.1, f32[6,3,2240]{2,1,0:T(4,128)} %mod_ref.1, bf16[2240,512]{1,0:T(8,128)(2,1)} %bitcast.6, bf16[3,1120,640]{2,1,0:T(8,128)(2,1)} %bitcast.5, bf16[1120,640]{1,0:T(8,128)(2,1)} %bitcast.7), custom_call_target="tpu_custom_call" | custom-call | tf_op jit(solution)/shard_map/pallas_call | solution.py:344
  33.4 2.3 %copy.7 = bf16[512,1120]{0,1:T(8,128)(2,1)} copy(bf16[512,1120]{0,1:T(8,128)(2,1)} %bitcast.4) | data formatting | bytes 2293760
